TPU v7x, 512 devices: a whole 4x4x16 slice. The times are simulated.
512 devices in a mesh: patch: 64 (over z_hi, x, y, core), head: 8 (over z_lo).
Axes of the slice: x: 4, y: 4, z: 16 (z_hi: 2, z_lo: 8; z = z_hi * 8 + z_lo), core: 2. Of those that a mesh axis runs over, the one named last changes fastest.
Arguments:
- query: bfloat16 [1536, 5120], P(('patch', 'head')), may hold values from -300 to 300
- delta_key: float32 [1536, 5120], P(('patch', 'head')), may hold values from -4 to 4
- delta_value: float32 [1536, 5120], P(('patch', 'head')), may hold values from -4 to 4
- base_key: bfloat16 [1536, 5120], P(None, 'head'), may hold values from -8 to 8
- base_value: bfloat16 [1536, 5120], P(None, 'head'), may hold values from -6 to 6
Outputs:
- attended: bfloat16 [1536, 5120], P(('patch', 'head'))
All inputs are finite; a program needn't handle non-finite values. Where the computation divides by a largest or mean magnitude, that divisor is 1e-20 or more.
Results may differ from a plain program's by a relative error of at most 0.04.
Values may be sent and summed in bfloat16 or wider, within the bound.
A program may use at most 64 MiB of HBM per device.

v0:
```python
import math

import jax
import jax.numpy as jnp
from jax import lax
from jax.sharding import PartitionSpec as P

HEAD_DIM = 128


def encode(delta, head_dim):
    rows_count, features = delta.shape
    blocks = delta.reshape(rows_count, features // head_dim, head_dim)
    scales = (jnp.max(jnp.abs(blocks), axis=2) + 1e-06).astype(jnp.bfloat16)
    levels = jnp.floor(127.0 * blocks / scales.astype(jnp.float32)[:, :, None] + 0.5)
    codes = jnp.clip(levels, -127.0, 127.0).astype(jnp.bfloat16)
    return (codes.reshape(rows_count, features), scales)


def decode(base, codes, scales, head_dim):
    rows_count, features = codes.shape
    head_count = features // head_dim
    rebuilt = base.astype(jnp.float32).reshape(rows_count, head_count, head_dim)
    steps_size = scales.astype(jnp.float32)[:, :, None] / 127.0
    rebuilt = (
        rebuilt + codes.astype(jnp.float32).reshape(rows_count, head_count, head_dim) * steps_size
    )
    return rebuilt.astype(jnp.bfloat16)


def absorb(carry, keys, values, queries):
    running_max, row_total, accum_out = carry
    factor = 1.0 / math.sqrt(queries.shape[2])
    scores = jnp.einsum("qhd,khd->hqk", queries, keys, preferred_element_type=jnp.float32) * factor
    new_peak = jnp.maximum(running_max, jnp.max(scores, axis=2))
    shrink = jnp.exp(running_max - new_peak)
    weights = jnp.exp(scores - new_peak[:, :, None])
    row_total = jnp.sum(weights, axis=2)
    accum_out = jnp.einsum(
        "hqk,khd->hqd", weights.astype(jnp.bfloat16), values, preferred_element_type=jnp.float32
    )
    return (new_peak, row_total, accum_out)


def on_device(query, delta_key, delta_value, base_key, base_value):
    head_dim = HEAD_DIM
    code_k, scale_k = encode(delta_key, head_dim)
    code_v, scale_v = encode(delta_value, head_dim)
    head_width = base_key.shape[1]
    local_heads = head_width // head_dim
    moved = (
        lax.all_to_all(query, "head", split_axis=1, concat_axis=0, tiled=True),
        lax.all_to_all(code_k, "head", split_axis=1, concat_axis=0, tiled=True),
        lax.all_to_all(code_v, "head", split_axis=1, concat_axis=0, tiled=True),
        lax.all_to_all(scale_k, "head", split_axis=1, concat_axis=0, tiled=True),
        lax.all_to_all(scale_v, "head", split_axis=1, concat_axis=0, tiled=True),
    )
    query_rows, codes_key, codes_value, scales_key, scales_value = moved
    query_count = query_rows.shape[0]
    queries = query_rows.reshape(query_count, local_heads, head_dim)
    start_carry = (
        jnp.full((local_heads, query_count), -1e30, jnp.float32),
        jnp.zeros((local_heads, query_count), jnp.float32),
        jnp.zeros((local_heads, query_count, head_dim), jnp.float32),
    )
    all_codes = (
        lax.all_gather(codes_key, "patch", axis=0, tiled=True),
        lax.all_gather(codes_value, "patch", axis=0, tiled=True),
        lax.all_gather(scales_key, "patch", axis=0, tiled=True),
        lax.all_gather(scales_value, "patch", axis=0, tiled=True),
    )
    codes_key, codes_value, scales_key, scales_value = all_codes
    keys = decode(base_key, codes_key, scales_key, head_dim)
    values = decode(base_value, codes_value, scales_value, head_dim)
    final_carry = absorb(start_carry, keys, values, queries)
    accum_out = final_carry[2] / final_carry[1][:, :, None]
    result_rows = accum_out.transpose(1, 0, 2).reshape(query_count, head_width).astype(jnp.bfloat16)
    return lax.all_to_all(result_rows, "head", split_axis=0, concat_axis=1, tiled=True)


def solution(mesh):
    in_specs = (
        P(("patch", "head"), None),
        P(("patch", "head"), None),
        P(("patch", "head"), None),
        P(None, "head"),
        P(None, "head"),
    )
    out_specs = P(("patch", "head"), None)
    return jax.shard_map(
        on_device, mesh=mesh, in_specs=in_specs, out_specs=out_specs, check_vma=False
    )
```

profile of v0, /device:TPU:1, one launch (start us, length us, event | category | flops | bytes accessed | tf_op | source)
XLA Modules:
  0.0 437.3 jit_solution(616833511221179346)
XLA Ops:
  6.5 0.9 abs_bitcast_fusion.1
  7.6 1.0 clamp_convert_fusion.1
  8.6 22.4 %all_to_all.102 = bf16[3,8,640]{2,0,1:T(4,128)(2,1)S(1)} all-to-all(bf16[3,8,640]{2,0,1:T(4,128)(2,1)S(1)} %bitcast.58), channel_id=1, replica_groups=mesh['patch'=64,'head'=8] {'head'}, dimensions={1} | all-to-all | bytes 61440 | tf_op jit(solution)/shard_map/all_to_all | solution.py:53
  31.0 0.6 all_to_all.79
  31.7 0.9 abs_bitcast_fusion
  32.8 1.0 clamp_convert_fusion
  33.8 11.9 %all_to_all.103 = bf16[3,8,640]{2,0,1:T(4,128)(2,1)S(1)} all-to-all(bf16[3,8,640]{2,0,1:T(4,128)(2,1)S(1)} %bitcast.59), channel_id=1, replica_groups=mesh['patch'=64,'head'=8] {'head'}, dimensions={1} | all-to-all | bytes 61440 | tf_op jit(solution)/shard_map/all_to_all | solution.py:54
  45.7 0.6 all_to_all.89
  46.5 0.6 copy.45
  47.1 3.3 all-to-all-start.1
  50.4 2.7 copy.42
  53.2 0.6 copy.55
  53.8 4.1 copy.52
  57.9 1.7 all-to-all-done.1
  59.6 7.5 %all-to-all-start.4 = ((bf16[3,8,5]{2,0,1:T(4,128)(2,1)}), bf16[3,8,5]{2,0,1:T(4,128)(2,1)S(1)}, u32[]{:S(2)}, u32[]{:S(2)}) async-start(bf16[3,8,5]{2,0,1:T(4,128)(2,1)} %copy.55), calls=%async_computation.4 | async-start | bytes 16384 | tf_op jit(solution)/shard_map/all_to_all | solution.py:56
  67.3 161.4 %all-gather = bf16[64,24,5]{1,2,0:T(8,128)(2,1)S(1)} all-gather(bf16[1,24,5]{1,2,0:T(8,128)(2,1)S(1)} %copy.63), channel_id=1, replica_groups=mesh['patch'=64,'head'=8] {'patch'}, dimensions={0}, use_global_device_ids=true | all-gather | bytes 15600 | tf_op jit(solution)/shard_map/all_gather | solution.py:69
  228.8 20.1 %all-to-all-start.2 = ((bf16[3,8,640]{2,0,1:T(4,128)(2,1)}), bf16[3,8,640]{2,0,1:T(4,128)(2,1)S(1)}, u32[]{:S(2)}, u32[]{:S(2)}) async-start(bf16[3,8,640]{2,0,1:T(4,128)(2,1)} %bitcast.5), calls=%async_computation.2 | async-start | bytes 81920 | tf_op jit(solution)/shard_map/all_to_all | solution.py:52
  249.0 146.5 %all-gather.1 = bf16[64,24,5]{1,2,0:T(8,128)(2,1)S(1)} all-gather(bf16[1,24,5]{1,2,0:T(8,128)(2,1)S(1)} %copy.64), channel_id=1, replica_groups=mesh['patch'=64,'head'=8] {'patch'}, dimensions={0}, use_global_device_ids=true | all-gather | bytes 15600 | tf_op jit(solution)/shard_map/all_gather | solution.py:70
  396.2 4.2 copy.44
  400.4 2.8 fusion.24
  403.5 4.4 %copy.54 = f32[1536,640]{0,1:T(8,128)} copy(bf16[1536,640]{1,0:T(8,128)(2,1)} %all-gather.7.cloned.1.call-done) | data formatting | bytes 5898240 | tf_op jit(solution)/shard_map/reshape | solution.py:26
  407.9 2.8 fusion.14
  410.8 19.1 %all_to_all.104 = bf16[8,3,640]{2,1,0:T(4,128)(2,1)S(1)} all-to-all(bf16[8,3,640]{2,1,0:T(4,128)(2,1)S(1)} %convert_element_type.84), channel_id=1, replica_groups=mesh['patch'=64,'head'=8] {'head'}, dimensions={0} | all-to-all | bytes 61440 | tf_op jit(solution)/shard_map/all_to_all | solution.py:78
  429.8 0.6 copy.82
  (35 shorter events, 1.9 us)
Async XLA Ops:
  6.5 389.6 %all-gather.5.cloned.1.call-start = ((), (), s32[]{:S(2)}) async-start(), calls=%async_computation.6 | async-start | bytes 1996800 | tf_op jit(solution)/shard_map/all_gather | solution.py:67
  31.7 371.8 %all-gather.7.cloned.1.call-start = ((), (), s32[]{:S(2)}) async-start(), calls=%async_computation.7 | async-start | bytes 1996800 | tf_op jit(solution)/shard_map/all_gather | solution.py:68
  47.1 12.5 %all-to-all-start.1 = ((bf16[3,8,5]{2,0,1:T(4,128)(2,1)}), bf16[3,8,5]{2,0,1:T(4,128)(2,1)S(1)}, u32[]{:S(2)}, u32[]{:S(2)}) async-start(bf16[3,8,5]{2,0,1:T(4,128)(2,1)} %copy.45), calls=%async_computation.1 | async-start | bytes 16384 | tf_op jit(solution)/shard_map/all_to_all | solution.py:55
  59.6 169.2 %all-to-all-start.4 = ((bf16[3,8,5]{2,0,1:T(4,128)(2,1)}), bf16[3,8,5]{2,0,1:T(4,128)(2,1)S(1)}, u32[]{:S(2)}, u32[]{:S(2)}) async-start(bf16[3,8,5]{2,0,1:T(4,128)(2,1)} %copy.55), calls=%async_computation.4 | async-start | bytes 16384 | tf_op jit(solution)/shard_map/all_to_all | solution.py:56
  228.8 167.3 %all-to-all-start.2 = ((bf16[3,8,640]{2,0,1:T(4,128)(2,1)}), bf16[3,8,640]{2,0,1:T(4,128)(2,1)S(1)}, u32[]{:S(2)}, u32[]{:S(2)}) async-start(bf16[3,8,640]{2,0,1:T(4,128)(2,1)} %bitcast.5), calls=%async_computation.2 | async-start | bytes 81920 | tf_op jit(solution)/shard_map/all_to_all | solution.py:52
  403.2 4.7 %copy-start = (bf16[1536,640]{0,1:T(8,128)(2,1)S(1)}, bf16[1536,640]{0,1:T(8,128)(2,1)}, u32[]{:S(2)}) copy-start(bf16[1536,640]{0,1:T(8,128)(2,1)} %copy.52) | copy-start | bytes 5898244
Sparse Core Ops, SparseCore 0:
  31.8 110.1 all-gather.4
  146.5 99.9 all-gather.6
where the time goes:
time: 439 us; the launch traced here: 437 us
  blocking collectives  361 us (82%)
  starting transfers between devices  31 us (7%)
  local copies, waits for them, and re-layouts  19.9 us (5%)
  between operations  13.6 us (3%)
  matrix products  5.59 us (1%)
    all_gather x1, blocking collectives, on_device(): lax.all_gather(scales_key, 'patch', axis=0, tiled=True)  161 us
    all_gather x1, blocking collectives, on_device(): lax.all_gather(scales_value, 'patch', axis=0, tiled=True)  146 us
    all_to_all x1, blocking collectives, on_device(): lax.all_to_all(code_k, 'head', split_axis=1, concat_axis=0, tiled=True)  22.4 us
    all_to_all x1, starting transfers between devices, on_device(): lax.all_to_all(query, 'head', split_axis=1, concat_axis=0, tiled=True)  20.1 us
    all_to_all x1, blocking collectives, on_device(): lax.all_to_all(result_rows, 'head', split_axis=0, concat_axis=1, tiled=True)  19.1 us
    all_to_all x1, blocking collectives, on_device(): lax.all_to_all(code_v, 'head', split_axis=1, concat_axis=0, tiled=True)  11.9 us
  transfers between devices with their start and end apart: 5, of which 1 were waited for; matrix products, arithmetic and copies ran while one was open for 4% of the time, Pallas kernels for 0%

commit v1 on v0

v1 whole, which is shorter than its diff:
```python
import math

import jax
import jax.numpy as jnp
from jax import lax
from jax.experimental import pallas as pl
from jax.experimental.pallas import tpu as pltpu
from jax.sharding import PartitionSpec as P

MESH = pl.DeviceIdType.MESH
F32 = jnp.float32
BF16 = jnp.bfloat16

HD = 128
NX, NY, NC = 4, 4, 2
NL = 8
NZ = 2 * NL
TOK = 3
ZT = TOK * NZ
HT = TOK * NL
YC = NY * NC
PLANE = NX * YC
MSG = 32
KEYS = NX * ZT
SLOTS = 128
OROWS = HD + 16
SCALE2 = math.log2(math.e) / math.sqrt(HD)

NT = (((1,), (1,)), ((), ()))


def kernel(
    q_ref, dk_ref, dv_ref, bk_ref, bv_ref, out_ref,
    stage, sbuf, rbuf, pmat, p2mat, bwin, bf32,
    kall, vall, qall, vt, obuf, orecv, fbuf, frecv, fstage, fout,
    bsem, zs, zr, ks, kr, vs, vr, qs, qr, osm, orm, fs, fr,
):
    p = lax.axis_index("patch")
    h = lax.axis_index("head")
    zh = lax.div(p, PLANE)
    xyc = lax.rem(p, PLANE)
    x = lax.div(xyc, YC)
    yc = lax.rem(xyc, YC)
    y = lax.div(yc, NC)
    core = lax.rem(yc, NC)
    z = zh * NL + h

    def zdev(z2):
        return (lax.div(z2, NL) * PLANE + xyc, lax.rem(z2, NL))

    def xdev(x2):
        return (zh * PLANE + x2 * YC + yc, h)

    def ydev(yc2):
        return (zh * PLANE + x * YC + yc2, h)

    barrier = pltpu.get_barrier_semaphore()

    @pl.loop(1, NZ)
    def _(k):
        pl.semaphore_signal(barrier, inc=1, device_id=zdev(lax.rem(z + k, NZ)), device_id_type=MESH)

    @pl.loop(1, NX)
    def _(k):
        pl.semaphore_signal(barrier, inc=1, device_id=xdev(lax.rem(x + k, NX)), device_id_type=MESH)

    @pl.loop(1, YC)
    def _(k):
        pl.semaphore_signal(barrier, inc=1, device_id=ydev(lax.rem(yc + k, YC)), device_id_type=MESH)

    base_copies = []
    for a, ref in enumerate((bk_ref, bv_ref)):
        for half in range(2):
            row0 = pl.multiple_of(lax.div(HT * (xyc + half * PLANE), 16) * 16, 16)
            rows = pl.ds(row0, 32)
            ab = pl.ds(pl.multiple_of(zh * (3 * HD), HD), 2 * HD)
            n = 2 * (2 * a + half)
            base_copies.append(pltpu.make_async_copy(
                ref.at[rows, ab], bwin.at[a, half, :, pl.ds(0, 2 * HD)], bsem.at[n]))
            base_copies.append(pltpu.make_async_copy(
                ref.at[rows, pl.ds(2 * HD, HD)], bwin.at[a, half, :, pl.ds(2 * HD, HD)], bsem.at[n + 1]))
    for copy in base_copies:
        copy.start()

    lane = lax.broadcasted_iota(jnp.int32, (TOK, HD), 1)
    stage[:, 30:32, :] = jnp.zeros((NZ, 2, HD), F32)

    def encode(ref, g):
        block = ref[:, g * HD:(g + 1) * HD]
        scale = (jnp.max(jnp.abs(block), axis=1, keepdims=True) + 1e-06).astype(BF16).astype(F32)
        levels = jnp.floor(127.0 * block / scale + 0.5)
        return jnp.clip(levels, -127.0, 127.0), scale

    for hd in range(NL):
        scales = [jnp.zeros((TOK, HD), F32), jnp.zeros((TOK, HD), F32)]
        for j in range(5):
            g = 5 * hd + j
            code_k, scale_k = encode(dk_ref, g)
            code_v, scale_v = encode(dv_ref, g)
            query = q_ref[:, g * HD:(g + 1) * HD].astype(F32)
            targets = ((0, j),) if j < 2 else (((0, 2), (1, 2)) if j == 2 else ((1, j - 3),))
            for zz, slot in targets:
                dst = zz * NL + hd
                for n, piece in ((slot, code_k), (3 + slot, code_v), (6 + slot, query)):
                    stage[dst, 3 * n:3 * n + 3, :] = piece
                scales[zz] = jnp.where(lane == slot, scale_k, scales[zz])
                scales[zz] = jnp.where(lane == 3 + slot, scale_v, scales[zz])
        for zz in range(2):
            dst = zz * NL + hd
            stage[dst, 27:30, :] = scales[zz]
            sbuf[dst] = stage[dst].astype(BF16)

    pl.semaphore_wait(barrier, (NZ - 1) + (NX - 1) + (YC - 1))

    def zcopy(z2, mine, theirs):
        return pltpu.make_async_remote_copy(
            src_ref=sbuf.at[z2], dst_ref=rbuf.at[mine], send_sem=zs.at[z2], recv_sem=zr.at[theirs],
            device_id=zdev(z2), device_id_type=MESH)

    @pl.loop(1, NZ)
    def _(k):
        zcopy(lax.rem(z + k, NZ), z, z).start()

    rbuf[z] = sbuf[z]

    col = lax.broadcasted_iota(jnp.int32, (1, NZ * MSG), 1)
    row_in = jnp.bitwise_and(col, MSG - 1)
    piece_of = jnp.right_shift(row_in * 43, 7)
    token_of = 3 * jnp.right_shift(col, 5) + row_in - 3 * piece_of
    key = token_of + ZT * piece_of
    for n in range(10):
        r = lax.broadcasted_iota(jnp.int32, (ZT, NZ * MSG), 0) + n * ZT
        pmat[n * ZT:(n + 1) * ZT, :] = jnp.where(r == key, 1.0, 0.0).astype(BF16)
    r = lax.broadcasted_iota(jnp.int32, (32, NZ * MSG), 0) + (8 * ZT + HT * zh)
    pmat[10 * ZT:10 * ZT + 32, :] = jnp.where(r == key, 1.0, 0.0).astype(BF16)

    r2 = lax.broadcasted_iota(jnp.int32, (NZ * 16, SLOTS), 0)
    s2 = lax.broadcasted_iota(jnp.int32, (NZ * 16, SLOTS), 1)
    owner = jnp.right_shift(r2, 4)
    rr = jnp.bitwise_and(r2, 15)
    slot_a = jnp.where(rr < 3, 3 * owner + rr, -1)
    slot_b = jnp.where((rr >= 8) & (rr < 11), ZT + 3 * owner + rr - 8, -1)
    near = (rr >= 4) & (rr < 7) & (jnp.right_shift(owner, 3) == zh)
    slot_c = jnp.where(near, 2 * ZT + 3 * jnp.bitwise_and(owner, 7) + rr - 4, -1)
    p2mat[...] = jnp.where((s2 == slot_a) | (s2 == slot_b) | (s2 == slot_c), 1.0, 0.0).astype(BF16)

    for copy in base_copies:
        copy.wait()
    bf32[...] = bwin[...].astype(F32)

    @pl.loop(1, NZ)
    def _(k):
        z2 = lax.rem(z + k, NZ)
        zcopy(z2, z, z2).wait_recv()

    arrived = rbuf[...].reshape(NZ * MSG, HD)

    def pick(first, rows):
        return jnp.dot(pmat[first:first + rows, :], arrived, preferred_element_type=F32)

    steps = pick(9 * ZT, ZT) / 127.0
    shift = pl.ds(pl.multiple_of(8 * lax.rem(xyc, 2), 8), HT)

    def decode(a, dest):
        for slot in range(3):
            codes = pick((3 * a + slot) * ZT, ZT)
            step = steps[:, 3 * a + slot:3 * a + slot + 1]
            base = jnp.concatenate(
                [bf32[a, half, shift, slot * HD:(slot + 1) * HD] for half in range(2)], axis=0)
            dest[slot, x] = (base + codes * step).astype(BF16)

    def xcopy(buf, x2, mine, theirs, ssem, rsem):
        return pltpu.make_async_remote_copy(
            src_ref=buf.at[:, mine], dst_ref=buf.at[:, mine], send_sem=ssem.at[x2], recv_sem=rsem.at[theirs],
            device_id=xdev(x2), device_id_type=MESH)

    def ycopy(src, dst, yc2, theirs, ssem, rsem):
        return pltpu.make_async_remote_copy(
            src_ref=src, dst_ref=dst, send_sem=ssem.at[yc2], recv_sem=rsem.at[theirs],
            device_id=ydev(yc2), device_id_type=MESH)

    decode(0, kall)

    @pl.loop(1, NX)
    def _(k):
        xcopy(kall, lax.rem(x + k, NX), x, x, ks, kr).start()

    qall[yc] = jnp.concatenate([pick(6 * ZT, 2 * ZT), pick(10 * ZT, 32)], axis=0).astype(BF16)

    @pl.loop(1, YC)
    def _(k):
        yc2 = lax.rem(yc + k, YC)
        ycopy(qall.at[yc], qall.at[yc], yc2, yc, qs, qr).start()

    decode(1, vall)

    @pl.loop(1, NX)
    def _(k):
        xcopy(vall, lax.rem(x + k, NX), x, x, vs, vr).start()

    @pl.loop(1, NX)
    def _(k):
        x2 = lax.rem(x + k, NX)
        xcopy(kall, x2, x2, x2, ks, kr).wait_recv()

    @pl.loop(1, NX)
    def _(k):
        x2 = lax.rem(x + k, NX)
        xcopy(vall, x2, x2, x2, vs, vr).wait_recv()

    eye = jnp.where(
        lax.broadcasted_iota(jnp.int32, (HD, HD), 0) == lax.broadcasted_iota(jnp.int32, (HD, HD), 1),
        1.0, 0.0).astype(BF16)
    for slot in range(3):
        values = vall[slot].reshape(KEYS, HD)
        vt[slot * HD:(slot + 1) * HD, :] = lax.dot_general(
            eye, values, NT, preferred_element_type=F32).astype(BF16)

    slot_lane = jnp.bitwise_and(lax.broadcasted_iota(jnp.int32, (1, NC * SLOTS), 1), SLOTS - 1)
    in_a, in_b = slot_lane < ZT, slot_lane < 2 * ZT
    stat_row = lax.broadcasted_iota(jnp.int32, (16, NC * SLOTS), 0)

    def choose(stacked, rows):
        return jnp.where(
            in_a, stacked[0:rows], jnp.where(in_b, stacked[rows:2 * rows], stacked[2 * rows:3 * rows]))

    def attend(y2):
        first = y2 * NC
        queries = qall[pl.ds(first, NC)].reshape(NC * SLOTS, HD)
        keys = kall[...].reshape(3 * KEYS, HD)
        scores = lax.dot_general(keys, queries, NT, preferred_element_type=F32)
        scores = choose(scores, KEYS) * SCALE2
        peak = jnp.max(scores, axis=0, keepdims=True)
        peak_hi = peak.astype(BF16).astype(F32)
        peak_lo = (peak - peak_hi).astype(BF16).astype(F32)
        weights = jnp.exp2(scores - (peak_hi + peak_lo))
        total = jnp.sum(weights, axis=0, keepdims=True)
        total_hi = total.astype(BF16).astype(F32)
        total_lo = total - total_hi
        mixed = jnp.dot(vt[...], weights.astype(BF16), preferred_element_type=F32)
        mixed = choose(mixed, HD).astype(BF16)
        stats = jnp.where(stat_row == 0, peak_hi, jnp.where(
            stat_row == 1, peak_lo, jnp.where(
                stat_row == 2, total_hi, jnp.where(stat_row == 3, total_lo, 0.0)))).astype(BF16)
        for c in range(NC):
            obuf[first + c, 0:HD, :] = mixed[:, c * SLOTS:(c + 1) * SLOTS]
            obuf[first + c, HD:OROWS, :] = stats[:, c * SLOTS:(c + 1) * SLOTS]

    def send_out(yc2):
        ycopy(obuf.at[yc2], orecv.at[yc], yc2, yc, osm, orm).start()

    def wait_queries(yc2):
        ycopy(qall.at[yc2], qall.at[yc2], yc2, yc2, qs, qr).wait_recv()

    wait_queries(y * NC + 1 - core)
    attend(y)
    send_out(y * NC + 1 - core)
    orecv[yc] = obuf[yc]

    @pl.loop(1, NY)
    def _(k):
        y2 = lax.rem(y + k, NY)
        for c in range(NC):
            wait_queries(y2 * NC + c)
        attend(y2)
        for c in range(NC):
            send_out(y2 * NC + c)

    @pl.loop(1, YC)
    def _(k):
        yc2 = lax.rem(yc + k, YC)
        ycopy(obuf.at[yc2], orecv.at[yc2], yc2, yc2, osm, orm).wait_recv()

    stats = [orecv[n, HD:OROWS, :].astype(F32) for n in range(YC)]
    peaks = [s[0:1] + s[1:2] for s in stats]
    top = peaks[0]
    for n in range(1, YC):
        top = jnp.maximum(top, peaks[n])
    parts = [jnp.exp2(peaks[n] - top) for n in range(YC)]
    total = jnp.zeros((1, SLOTS), F32)
    for n in range(YC):
        total = total + parts[n] * (stats[n][2:3] + stats[n][3:4])
    joined = jnp.zeros((HD, SLOTS), F32)
    for n in range(YC):
        joined = joined + orecv[n, 0:HD, :].astype(F32) * parts[n]
    joined = (joined / total).astype(BF16)
    owned = lax.dot_general(p2mat[...], joined, NT, preferred_element_type=F32)
    fbuf[...] = owned.astype(BF16).reshape(NZ, 16, HD)

    def fcopy(z2, mine, theirs):
        return pltpu.make_async_remote_copy(
            src_ref=fbuf.at[z2], dst_ref=frecv.at[mine], send_sem=fs.at[z2], recv_sem=fr.at[theirs],
            device_id=zdev(z2), device_id_type=MESH)

    @pl.loop(1, NZ)
    def _(k):
        fcopy(lax.rem(z + k, NZ), z, z).start()

    frecv[z] = fbuf[z]

    @pl.loop(1, NZ)
    def _(k):
        z2 = lax.rem(z + k, NZ)
        zcopy(z2, z, z2).wait_send()

    @pl.loop(1, NX)
    def _(k):
        x2 = lax.rem(x + k, NX)
        xcopy(kall, x2, x, x2, ks, kr).wait_send()
        xcopy(vall, x2, x, x2, vs, vr).wait_send()

    @pl.loop(1, YC)
    def _(k):
        yc2 = lax.rem(yc + k, YC)
        ycopy(qall.at[yc], qall.at[yc], yc2, yc2, qs, qr).wait_send()
        ycopy(obuf.at[yc2], orecv.at[yc], yc2, yc2, osm, orm).wait_send()

    @pl.loop(1, NZ)
    def _(k):
        z2 = lax.rem(z + k, NZ)
        fcopy(z2, z2, z2).wait_recv()

    fstage[...] = frecv[...].astype(F32)
    for n in range(NZ):
        g = 5 * (n % NL) + 3 * (n // NL)
        fout[:, g * HD:(g + 1) * HD] = fstage[n, 0:3, :]
        fout[:, (g + 1) * HD:(g + 2) * HD] = fstage[n, 8:11, :]
    for hd in range(NL):
        g = 5 * hd + 2
        fout[:, g * HD:(g + 1) * HD] = fstage[zh * NL + hd, 4:7, :]
    out_ref[...] = fout[...].astype(BF16)

    @pl.loop(1, NZ)
    def _(k):
        z2 = lax.rem(z + k, NZ)
        fcopy(z2, z, z2).wait_send()


def on_device(query, delta_key, delta_value, base_key, base_value):
    vmem = pl.BlockSpec(memory_space=pltpu.VMEM)
    hbm = pl.BlockSpec(memory_space=pl.ANY)
    dma = pltpu.SemaphoreType.DMA
    return pl.pallas_call(
        kernel,
        out_shape=jax.ShapeDtypeStruct(query.shape, BF16),
        in_specs=[vmem, vmem, vmem, hbm, hbm],
        out_specs=vmem,
        scratch_shapes=[
            pltpu.VMEM((NZ, MSG, HD), F32),
            pltpu.VMEM((NZ, MSG, HD), BF16),
            pltpu.VMEM((NZ, MSG, HD), BF16),
            pltpu.VMEM((10 * ZT + 32, NZ * MSG), BF16),
            pltpu.VMEM((NZ * 16, SLOTS), BF16),
            pltpu.VMEM((2, 2, 32, 3 * HD), BF16),
            pltpu.VMEM((2, 2, 32, 3 * HD), F32),
            pltpu.VMEM((3, NX, ZT, HD), BF16),
            pltpu.VMEM((3, NX, ZT, HD), BF16),
            pltpu.VMEM((YC, SLOTS, HD), BF16),
            pltpu.VMEM((3 * HD, KEYS), BF16),
            pltpu.VMEM((YC, OROWS, SLOTS), BF16),
            pltpu.VMEM((YC, OROWS, SLOTS), BF16),
            pltpu.VMEM((NZ, 16, HD), BF16),
            pltpu.VMEM((NZ, 16, HD), BF16),
            pltpu.VMEM((NZ, 16, HD), F32),
            pltpu.VMEM(query.shape, F32),
            dma((8,)), dma((NZ,)), dma((NZ,)), dma((NX,)), dma((NX,)), dma((NX,)), dma((NX,)),
            dma((YC,)), dma((YC,)), dma((YC,)), dma((YC,)), dma((NZ,)), dma((NZ,)),
        ],
        compiler_params=pltpu.CompilerParams(
            collective_id=0, has_side_effects=True, vmem_limit_bytes=60 * 1024 * 1024),
    )(query, delta_key, delta_value, base_key, base_value)


def solution(mesh):
    rows = P(("patch", "head"), None)
    cols = P(None, "head")
    return jax.shard_map(
        on_device, mesh=mesh, in_specs=(rows, rows, rows, cols, cols), out_specs=rows, check_vma=False)
```

time: 439 us -> 51.7 us (0.12)
  blocking collectives: 361 us -> 0 us
  Pallas kernels: 0 us -> 50.1 us
  starting transfers between devices: 31 us -> 0 us
  local copies, waits for them, and re-layouts: 19.9 us -> 1.41 us
  between operations: 13.6 us -> 0.01 us
  matrix products: 5.59 us -> 0 us
    all_gather x2 -> x0, blocking collectives: 308 us -> none  [the longest x1 161 us: on_device(): lax.all_gather(scales_key, 'patch', axis=0, tiled=True)]
    all_to_all x3 -> x0, blocking collectives: 53.4 us -> none  [the longest x1 22.4 us: on_device(): lax.all_to_all(code_k, 'head', split_axis=1, concat_axis=0, tiled=True)]
    pallas_call x0 -> x1, Pallas kernels: none -> 50.1 us  [on_device(): pl.pallas_call(kernel, out_shape=jax.ShapeDtypeStruct(query.shape, BF16),...]
    all_to_all x3 -> x0, starting transfers between devices: 30.9 us -> none  [the longest x1 20.1 us: on_device(): lax.all_to_all(query, 'head', split_axis=1, concat_axis=0, tiled=True)]
    reshape x3 -> x0, local copies, waits for them, and re-layouts: 8.67 us -> none  [the longest x2 8.63 us: decode(): codes.astype(jnp.float32).reshape(rows_count, head_count, head_dim)]
    unnamed x11 -> x1, local copies, waits for them, and re-layouts: 7.77 us -> 1.41 us
    dot_general x2 -> x0, matrix products: 5.59 us -> none  [the longest x1 2.8 us: absorb(): jnp.einsum('hqk,khd->hqd', weights.astype(jnp.bfloat16), values, preferre...]
  transfers between devices with their start and end apart: 5 -> 0, of which waited for: 1 -> 0; matrix products, arithmetic and copies ran while one was open for 4% -> 0% of each run, Pallas kernels for 0% -> 0%
where the time goes in v1:
time: 51.7 us; the launch traced here: 51.5 us
  Pallas kernels  50.1 us (97%)
  local copies, waits for them, and re-layouts  1.41 us (3%)
    pallas_call x1, Pallas kernels, on_device(): pl.pallas_call(kernel, out_shape=jax.ShapeDtypeStruct(query.shape, BF16),...  50.1 us
    unnamed x1, local copies, waits for them, and re-layouts  1.41 us

profile of v1, /device:TPU:1, one launch (start us, length us, event | category | flops | bytes accessed | tf_op | source)
XLA Modules:
  0.0 51.5 jit_solution(9254713884412101203)
XLA Ops:
  0.0 50.1 %shard_map.55 = bf16[3,5120]{1,0:T(4,128)(2,1)} custom-call(bf16[3,5120]{1,0:T(4,128)(2,1)} %q_ref.1, f32[3,5120]{1,0:T(4,128)} %dk_ref.1, f32[3,5120]{1,0:T(4,128)} %dv_ref.1, bf16[1536,640]{1,0:T(8,128)(2,1)} %bk_ref.1, bf16[1536,640]{1,0:T(8,128)(2,1)} %bv_ref.1), custom_call_target="tpu_custom_call" | custom-call | tf_op jit(solution)/shard_map/pallas_call | solution.py:343
  50.1 1.4 %copy.7 = bf16[3,5120]{1,0:T(4,128)(2,1)} copy(bf16[3,5120]{1,0:T(4,128)(2,1)} %shard_map.55) | data formatting | bytes 61440

commit v2 on v0

v2 whole, which is shorter than its diff:
```python
import math

import jax
import jax.numpy as jnp
from jax import lax
from jax.experimental import pallas as pl
from jax.experimental.pallas import tpu as pltpu
from jax.sharding import PartitionSpec as P

MESH = pl.DeviceIdType.MESH
F32 = jnp.float32
BF16 = jnp.bfloat16

HD = 128
NX, NY, NC = 4, 4, 2
NL = 8
NZ = 2 * NL
GH = 5
GW = GH * HD
TOK = 3
ZT = TOK * NZ
HT = TOK * NL
NXY = NX * NY
PLANE = NXY * NC
KEYS = NC * ZT
SLOTS = 128
OROWS = HD + 16
REACH = (4, -3, 3, -2, 2, -1, 1)
SCALE2 = math.log2(math.e) / math.sqrt(HD)

NT = (((1,), (1,)), ((), ()))


def iota(shape, dim):
    return lax.broadcasted_iota(jnp.int32, shape, dim)


def one_hot(cond):
    return jnp.where(cond, 1.0, 0.0).astype(BF16)


def third(n):
    return jnp.right_shift(n * 43, 7)


def slot_of(r):
    rr = jnp.bitwise_and(r, 15)
    j = third(rr)
    slot = HT * j + TOK * jnp.right_shift(r, 4) + rr - 3 * j
    return jnp.where(rr < 15, slot, -1)


def kernel(
    q_ref, dk_ref, dv_ref, bk_ref, bv_ref, out_ref,
    stage, qstage, sbuf, qsend, rbuf, qrecv, pmat, bwin, bf32,
    kall, vall, qall, vt, obuf, orecv, fbuf, frecv, fstage, fout,
    bsem, zs, zr, ws, wr, cs, cr, qs, qr, osm, orm, fs, fr,
):
    p = lax.axis_index("patch")
    h = lax.axis_index("head")
    zh = lax.div(p, PLANE)
    xyc = lax.rem(p, PLANE)
    xy = lax.div(xyc, NC)
    core = lax.rem(xyc, NC)
    z = zh * NL + h

    def zdev(z2):
        return (lax.div(z2, NL) * PLANE + xyc, lax.rem(z2, NL))

    def pdev(xy2):
        return (zh * PLANE + xy2 * NC + core, h)

    def zfar(k):
        half = lax.div(k + 1, 2)
        return lax.rem(z + NL + (2 * lax.rem(k, 2) - 1) * half + NZ, NZ)

    def near(d):
        return lax.rem(z + d + NZ, NZ)

    def cdev():
        return (zh * PLANE + xy * NC + 1 - core, h)

    barrier = pltpu.get_barrier_semaphore()

    @pl.loop(0, NZ - 1)
    def _(k):
        pl.semaphore_signal(barrier, inc=1, device_id=zdev(zfar(k)), device_id_type=MESH)

    @pl.loop(1, NXY)
    def _(k):
        pl.semaphore_signal(barrier, inc=1, device_id=pdev(lax.rem(xy + k, NXY)), device_id_type=MESH)

    pl.semaphore_signal(barrier, inc=1, device_id=cdev(), device_id_type=MESH)

    base_copies = []
    for a, ref in enumerate((bk_ref, bv_ref)):
        for half in range(2):
            row0 = pl.multiple_of(lax.div(HT * (xyc + half * PLANE), 16) * 16, 16)
            base_copies.append(pltpu.make_async_copy(
                ref.at[pl.ds(row0, 32)], bwin.at[a, half], bsem.at[2 * a + half]))
    for copy in base_copies:
        copy.start()

    lane = iota((TOK, HD), 1)
    sub = iota((TOK, HD), 0)
    qstage[:, 15:16, :] = jnp.zeros((NL, 1, HD), F32)

    def encode(ref, g):
        block = ref[:, g * HD:(g + 1) * HD]
        scale = (jnp.max(jnp.abs(block), axis=1, keepdims=True) + 1e-06).astype(BF16).astype(F32)
        levels = jnp.floor(127.0 * block / scale + 0.5)
        return jnp.clip(levels, -127.0, 127.0), scale

    for hd in range(NL):
        for a, ref in enumerate((dk_ref, dv_ref)):
            scales = jnp.zeros((TOK, HD), F32)
            for j in range(GH):
                code, scale = encode(ref, GH * hd + j)
                stage[hd, 16 * a + 3 * j:16 * a + 3 * j + 3, :] = code
                scales = jnp.where(lane == 3 * j + sub, scale, scales)
            stage[hd, 16 * a + 15:16 * a + 16, :] = jnp.sum(scales, axis=0, keepdims=True)
        sbuf[hd] = stage[hd].astype(BF16)

    for hd in range(NL):
        for j in range(GH):
            g = GH * hd + j
            qstage[hd, 3 * j:3 * j + 3, :] = q_ref[:, g * HD:(g + 1) * HD].astype(F32)
    qsend[...] = qstage[...].astype(BF16)

    pl.semaphore_wait(barrier, (NZ - 1) + (NXY - 1) + 1)

    def zcopy(z2, mine, theirs):
        return pltpu.make_async_remote_copy(
            src_ref=sbuf.at[lax.rem(z2, NL)], dst_ref=rbuf.at[mine], send_sem=zs.at[z2], recv_sem=zr.at[theirs],
            device_id=zdev(z2), device_id_type=MESH)

    def wcopy(d):
        i, z2 = d + 3, near(-d)
        return pltpu.make_async_remote_copy(
            src_ref=qsend.at[lax.rem(z2, NL)], dst_ref=qrecv.at[i], send_sem=ws.at[i], recv_sem=wr.at[i],
            device_id=zdev(z2), device_id_type=MESH)

    @pl.loop(0, NZ - 1)
    def _(k):
        zcopy(zfar(k), z, z).start()

    for d in REACH:
        wcopy(d).start()

    rbuf[z] = sbuf[h]
    qrecv[3] = qsend[h]

    col = iota((1, NZ * 32), 1)
    src = jnp.right_shift(col, 5)
    row32 = jnp.bitwise_and(col, 31)
    row16 = jnp.bitwise_and(col, 15)
    kind = jnp.right_shift(row32, 4)
    j_of = third(row16)
    key = kind * (GH * ZT) + ZT * j_of + TOK * src + row16 - 3 * j_of
    key = jnp.where(row16 < 15, key, -1)
    for n in range(2 * GH):
        pmat[n * ZT:(n + 1) * ZT, :] = one_hot(iota((ZT, NZ * 32), 0) + n * ZT == key)
    token = iota((ZT, NZ * 32), 0) - TOK * src
    mine = (token >= 0) & (token < TOK)
    for a in range(2):
        pmat[(2 * GH + a) * ZT:(2 * GH + a + 1) * ZT, :] = one_hot(mine & (row32 == 16 * a + 15))
    to_slots = one_hot(iota((SLOTS, NL * 16), 0) == slot_of(iota((SLOTS, NL * 16), 1)))
    to_owners = one_hot(slot_of(iota((NL * 16, SLOTS), 0)) == iota((NL * 16, SLOTS), 1))

    for d in REACH:
        wcopy(d).wait_recv()
    qall[xy] = jnp.dot(
        to_slots, qrecv[...].reshape(NL * 16, HD), preferred_element_type=F32).astype(BF16)

    def pcopy(src, dst, xy2, theirs, ssem, rsem):
        return pltpu.make_async_remote_copy(
            src_ref=src, dst_ref=dst, send_sem=ssem.at[xy2], recv_sem=rsem.at[theirs],
            device_id=pdev(xy2), device_id_type=MESH)

    @pl.loop(1, NXY)
    def _(k):
        xy2 = lax.rem(xy + k, NXY)
        pcopy(qall.at[xy], qall.at[xy], xy2, xy, qs, qr).start()

    for copy in base_copies:
        copy.wait()
    bf32[...] = bwin[...].astype(F32)

    @pl.loop(0, NZ - 1)
    def _(k):
        z2 = zfar(NZ - 2 - k)
        zcopy(z2, z, z2).wait_recv()

    arrived = rbuf[...].reshape(NZ * 32, HD)
    scales = jnp.dot(pmat[2 * GH * ZT:, :], arrived, preferred_element_type=F32)
    token_in = iota((ZT, HD), 0)
    lane_of = iota((ZT, HD), 1) - (token_in - 3 * third(token_in))
    picked = [
        jnp.where(lane_of == 3 * j, scales[a * ZT:(a + 1) * ZT], 0.0).astype(BF16)
        for a in range(2) for j in range(GH)]
    steps = jnp.dot(
        jnp.concatenate(picked, axis=0), jnp.ones((HD, HD), BF16), preferred_element_type=F32) / 127.0
    shift = pl.ds(pl.multiple_of(8 * lax.rem(xyc, 2), 8), HT)

    def decode(a, j, codes):
        n = a * GH + j
        base = jnp.concatenate(
            [bf32[a, half, shift, j * HD:(j + 1) * HD] for half in range(2)], axis=0)
        return (base + codes[j * ZT:(j + 1) * ZT] * steps[n * ZT:(n + 1) * ZT]).astype(BF16)

    def ccopy(a, mine, theirs):
        buf = (kall, vall)[a]
        return pltpu.make_async_remote_copy(
            src_ref=buf.at[:, mine], dst_ref=buf.at[:, mine], send_sem=cs.at[a], recv_sem=cr.at[a],
            device_id=cdev(), device_id_type=MESH)

    for a, buf in enumerate((kall, vall)):
        codes = jnp.dot(pmat[a * GH * ZT:(a + 1) * GH * ZT, :], arrived, preferred_element_type=F32)
        for j in range(GH):
            buf[j, core] = decode(a, j, codes)
        ccopy(a, core, core).start()
    for a in range(2):
        ccopy(a, core, core).wait_recv()

    eye = one_hot(iota((HD, HD), 0) == iota((HD, HD), 1))
    vt[...] = lax.dot_general(
        eye, vall[...].reshape(GH * KEYS, HD), NT, preferred_element_type=F32).astype(BF16)

    slot_lane = jnp.bitwise_and(iota((1, 2 * SLOTS), 1), SLOTS - 1)
    stat_row = iota((16, 2 * SLOTS), 0)

    def attend(m):
        queries = qall[pl.ds(2 * m, 2)].reshape(2 * SLOTS, HD)
        stacked = lax.dot_general(
            kall[...].reshape(GH * KEYS, HD), queries, NT, preferred_element_type=F32)
        scores = stacked[(GH - 1) * KEYS:]
        for j in range(GH - 2, -1, -1):
            scores = jnp.where(slot_lane < HT * (j + 1), stacked[j * KEYS:(j + 1) * KEYS], scores)
        scores = scores * SCALE2
        peak = jnp.max(scores, axis=0, keepdims=True)
        peak_hi = peak.astype(BF16).astype(F32)
        peak_lo = (peak - peak_hi).astype(BF16).astype(F32)
        weights = jnp.exp2(scores - (peak_hi + peak_lo))
        total = jnp.sum(weights, axis=0, keepdims=True)
        total_hi = total.astype(BF16).astype(F32)
        total_lo = total - total_hi
        by_head = []
        for j in range(GH):
            in_head = slot_lane >= HT * j
            if j < GH - 1:
                in_head = in_head & (slot_lane < HT * (j + 1))
            by_head.append(jnp.where(in_head, weights, 0.0).astype(BF16))
        mixed = jnp.dot(
            vt[...], jnp.concatenate(by_head, axis=0), preferred_element_type=F32).astype(BF16)
        stats = jnp.where(stat_row == 0, peak_hi, jnp.where(
            stat_row == 1, peak_lo, jnp.where(
                stat_row == 2, total_hi, jnp.where(stat_row == 3, total_lo, 0.0)))).astype(BF16)
        for c in range(2):
            obuf[2 * m + c, 0:HD, :] = mixed[:, c * SLOTS:(c + 1) * SLOTS]
            obuf[2 * m + c, HD:OROWS, :] = stats[:, c * SLOTS:(c + 1) * SLOTS]

    pairs = NXY // 2

    @pl.loop(0, pairs)
    def _(k):
        turn = (2 * lax.rem(k, 2) - 1) * lax.div(k + 1, 2)
        m = lax.rem(lax.div(xy, 2) + pairs // 2 + turn + pairs, pairs)
        for c in range(2):
            tile = 2 * m + c

            @pl.when(tile != xy)
            def _():
                pcopy(qall.at[tile], qall.at[tile], tile, tile, qs, qr).wait_recv()

        attend(m)
        for c in range(2):
            tile = 2 * m + c

            @pl.when(tile != xy)
            def _():
                pcopy(obuf.at[tile], orecv.at[xy], tile, xy, osm, orm).start()

            @pl.when(tile == xy)
            def _():
                orecv[tile] = obuf[tile]

    @pl.loop(1, NXY)
    def _(k):
        xy2 = lax.rem(xy + k, NXY)
        pcopy(obuf.at[xy2], orecv.at[xy2], xy2, xy2, osm, orm).wait_recv()

    stats = [orecv[n, HD:OROWS, :].astype(F32) for n in range(NXY)]
    peaks = [s[0:1] + s[1:2] for s in stats]
    top = peaks[0]
    for n in range(1, NXY):
        top = jnp.maximum(top, peaks[n])
    parts = [jnp.exp2(peaks[n] - top) for n in range(NXY)]
    total = jnp.zeros((1, SLOTS), F32)
    for n in range(NXY):
        total = total + parts[n] * (stats[n][2:3] + stats[n][3:4])
    joined = jnp.zeros((HD, SLOTS), F32)
    for n in range(NXY):
        joined = joined + orecv[n, 0:HD, :].astype(F32) * parts[n]
    joined = (joined / total).astype(BF16)
    owned = lax.dot_general(to_owners, joined, NT, preferred_element_type=F32)
    fbuf[...] = owned.astype(BF16).reshape(NL, 16, HD)

    def fcopy(d, theirs):
        i, z2 = d + 3, near(d)
        return pltpu.make_async_remote_copy(
            src_ref=fbuf.at[i], dst_ref=frecv.at[h], send_sem=fs.at[i], recv_sem=fr.at[theirs],
            device_id=zdev(z2), device_id_type=MESH)

    for d in REACH:
        fcopy(d, h).start()

    frecv[h] = fbuf[3]

    @pl.loop(0, NZ - 1)
    def _(k):
        zcopy(zfar(k), z, z).wait_send()

    for d in REACH:
        wcopy(d).wait_send()

    for a in range(2):
        ccopy(a, core, core).wait_send()

    @pl.loop(1, NXY)
    def _(k):
        xy2 = lax.rem(xy + k, NXY)
        pcopy(qall.at[xy], qall.at[xy], xy2, xy2, qs, qr).wait_send()
        pcopy(obuf.at[xy2], orecv.at[xy], xy2, xy2, osm, orm).wait_send()

    @pl.loop(1, NL)
    def _(k):
        h2 = lax.rem(h + k, NL)
        pltpu.make_async_remote_copy(
            src_ref=fbuf.at[0], dst_ref=frecv.at[h2], send_sem=fs.at[0], recv_sem=fr.at[h2],
            device_id=zdev(near(1)), device_id_type=MESH).wait_recv()

    fstage[...] = frecv[...].astype(F32)
    for hd in range(NL):
        for j in range(GH):
            g = GH * hd + j
            fout[:, g * HD:(g + 1) * HD] = fstage[hd, 3 * j:3 * j + 3, :]
    out_ref[...] = fout[...].astype(BF16)

    for d in REACH:
        fcopy(d, h).wait_send()


def on_device(query, delta_key, delta_value, base_key, base_value):
    vmem = pl.BlockSpec(memory_space=pltpu.VMEM)
    hbm = pl.BlockSpec(memory_space=pl.ANY)
    dma = pltpu.SemaphoreType.DMA
    return pl.pallas_call(
        kernel,
        out_shape=jax.ShapeDtypeStruct(query.shape, BF16),
        in_specs=[vmem, vmem, vmem, hbm, hbm],
        out_specs=vmem,
        scratch_shapes=[
            pltpu.VMEM((NL, 32, HD), F32),
            pltpu.VMEM((NL, 16, HD), F32),
            pltpu.VMEM((NL, 32, HD), BF16),
            pltpu.VMEM((NL, 16, HD), BF16),
            pltpu.VMEM((NZ, 32, HD), BF16),
            pltpu.VMEM((NL, 16, HD), BF16),
            pltpu.VMEM(((2 * GH + 2) * ZT, NZ * 32), BF16),
            pltpu.VMEM((2, 2, 32, GW), BF16),
            pltpu.VMEM((2, 2, 32, GW), F32),
            pltpu.VMEM((GH, NC, ZT, HD), BF16),
            pltpu.VMEM((GH, NC, ZT, HD), BF16),
            pltpu.VMEM((NXY, SLOTS, HD), BF16),
            pltpu.VMEM((HD, GH * KEYS), BF16),
            pltpu.VMEM((NXY, OROWS, SLOTS), BF16),
            pltpu.VMEM((NXY, OROWS, SLOTS), BF16),
            pltpu.VMEM((NL, 16, HD), BF16),
            pltpu.VMEM((NL, 16, HD), BF16),
            pltpu.VMEM((NL, 16, HD), F32),
            pltpu.VMEM(query.shape, F32),
            dma((4,)), dma((NZ,)), dma((NZ,)), dma((NL,)), dma((NL,)), dma((2,)), dma((2,)),
            dma((NXY,)), dma((NXY,)), dma((NXY,)), dma((NXY,)), dma((NL,)), dma((NL,)),
        ],
        compiler_params=pltpu.CompilerParams(
            collective_id=0, has_side_effects=True, vmem_limit_bytes=60 * 1024 * 1024),
    )(query, delta_key, delta_value, base_key, base_value)


def solution(mesh):
    rows = P(("patch", "head"), None)
    cols = P(None, "head")
    return jax.shard_map(
        on_device, mesh=mesh, in_specs=(rows, rows, rows, cols, cols), out_specs=rows, check_vma=False)
```

time: 439 us -> 50.5 us (0.12)
  the two profiles are of different devices: /device:TPU:1 before, /device:TPU:2 now
where the time goes in v2:
time: 50.5 us; the launch traced here: 50.3 us
  Pallas kernels  48.9 us (97%)
  local copies, waits for them, and re-layouts  1.41 us (3%)
    pallas_call x1, Pallas kernels, on_device(): pl.pallas_call(kernel, out_shape=jax.ShapeDtypeStruct(query.shape, BF16),...  48.9 us
    unnamed x1, local copies, waits for them, and re-layouts  1.41 us

profile of v2, /device:TPU:2, one launch (start us, length us, event | category | flops | bytes accessed | tf_op | source)
XLA Modules:
  0.0 50.3 jit_solution(17676810161319341599)
XLA Ops:
  0.0 48.9 %shard_map.55 = bf16[3,5120]{1,0:T(4,128)(2,1)} custom-call(bf16[3,5120]{1,0:T(4,128)(2,1)} %q_ref.1, f32[3,5120]{1,0:T(4,128)} %dk_ref.1, f32[3,5120]{1,0:T(4,128)} %dv_ref.1, bf16[1536,640]{1,0:T(8,128)(2,1)} %bk_ref.1, bf16[1536,640]{1,0:T(8,128)(2,1)} %bv_ref.1), custom_call_target="tpu_custom_call" | custom-call | tf_op jit(solution)/shard_map/pallas_call | solution.py:357
  48.9 1.4 %copy.7 = bf16[3,5120]{1,0:T(4,128)(2,1)} copy(bf16[3,5120]{1,0:T(4,128)(2,1)} %shard_map.55) | data formatting | bytes 61440

commit v3 on v2

--- a/solution.py
+++ b/solution.py
@@ -53,8 +53,8 @@
 def kernel(
     q_ref, dk_ref, dv_ref, bk_ref, bv_ref, out_ref,
     stage, qstage, sbuf, qsend, rbuf, qrecv, pmat, bwin, bf32,
-    kall, vall, qall, vt, obuf, orecv, fbuf, frecv, fstage, fout,
-    bsem, zs, zr, ws, wr, cs, cr, qs, qr, osm, orm, fs, fr,
+    kall, vall, qall, vt, obuf, orecv, fbuf, frecv, fstage, fout, q_in, dk_in, dv_in,
+    isem, bsem, zs, zr, ws, wr, cs, cr, qs, qr, osm, orm, fs, fr,
 ):
     p = lax.axis_index("patch")
     h = lax.axis_index("head")
@@ -67,6 +67,13 @@
     def zdev(z2):
         return (lax.div(z2, NL) * PLANE + xyc, lax.rem(z2, NL))
 
+    def pfar(k):
+        turn_x = lax.div(k, NY)
+        turn_y = lax.rem(k, NY)
+        x2 = lax.rem(lax.div(xy, NY) + NX // 2 + (2 * lax.rem(turn_x, 2) - 1) * lax.div(turn_x + 1, 2) + NX, NX)
+        y2 = lax.rem(lax.rem(xy, NY) + NY // 2 + (2 * lax.rem(turn_y, 2) - 1) * lax.div(turn_y + 1, 2) + NY, NY)
+        return x2 * NY + y2
+
     def pdev(xy2):
         return (zh * PLANE + xy2 * NC + core, h)
 
@@ -98,11 +105,18 @@
             row0 = pl.multiple_of(lax.div(HT * (xyc + half * PLANE), 16) * 16, 16)
             base_copies.append(pltpu.make_async_copy(
                 ref.at[pl.ds(row0, 32)], bwin.at[a, half], bsem.at[2 * a + half]))
+    in_copies = [
+        pltpu.make_async_copy(src, dst, isem.at[n])
+        for n, (src, dst) in enumerate(((dk_ref, dk_in), (dv_ref, dv_in), (q_ref, q_in)))]
+    for copy in in_copies:
+        copy.start()
     for copy in base_copies:
         copy.start()
 
     lane = iota((TOK, HD), 1)
     sub = iota((TOK, HD), 0)
+    for copy in in_copies:
+        copy.wait()
     qstage[:, 15:16, :] = jnp.zeros((NL, 1, HD), F32)
 
     def encode(ref, g):
@@ -112,7 +126,7 @@
         return jnp.clip(levels, -127.0, 127.0), scale
 
     for hd in range(NL):
-        for a, ref in enumerate((dk_ref, dv_ref)):
+        for a, ref in enumerate((dk_in, dv_in)):
             scales = jnp.zeros((TOK, HD), F32)
             for j in range(GH):
                 code, scale = encode(ref, GH * hd + j)
@@ -124,7 +138,7 @@
     for hd in range(NL):
         for j in range(GH):
             g = GH * hd + j
-            qstage[hd, 3 * j:3 * j + 3, :] = q_ref[:, g * HD:(g + 1) * HD].astype(F32)
+            qstage[hd, 3 * j:3 * j + 3, :] = q_in[:, g * HD:(g + 1) * HD].astype(F32)
     qsend[...] = qstage[...].astype(BF16)
 
     pl.semaphore_wait(barrier, (NZ - 1) + (NXY - 1) + 1)
@@ -140,12 +154,12 @@
             src_ref=qsend.at[lax.rem(z2, NL)], dst_ref=qrecv.at[i], send_sem=ws.at[i], recv_sem=wr.at[i],
             device_id=zdev(z2), device_id_type=MESH)
 
-    @pl.loop(0, NZ - 1)
-    def _(k):
-        zcopy(zfar(k), z, z).start()
-
     for d in REACH:
         wcopy(d).start()
+
+    @pl.loop(0, NZ - 1)
+    def _(k):
+        zcopy(zfar(k), z, z).start()
 
     rbuf[z] = sbuf[h]
     qrecv[3] = qsend[h]
@@ -177,10 +191,9 @@
             src_ref=src, dst_ref=dst, send_sem=ssem.at[xy2], recv_sem=rsem.at[theirs],
             device_id=pdev(xy2), device_id_type=MESH)
 
-    @pl.loop(1, NXY)
-    def _(k):
-        xy2 = lax.rem(xy + k, NXY)
-        pcopy(qall.at[xy], qall.at[xy], xy2, xy, qs, qr).start()
+    @pl.loop(0, NXY - 1)
+    def _(k):
+        pcopy(qall.at[xy], qall.at[xy], pfar(k), xy, qs, qr).start()
 
     for copy in base_copies:
         copy.wait()
@@ -357,7 +370,7 @@
     return pl.pallas_call(
         kernel,
         out_shape=jax.ShapeDtypeStruct(query.shape, BF16),
-        in_specs=[vmem, vmem, vmem, hbm, hbm],
+        in_specs=[hbm] * 5,
         out_specs=vmem,
         scratch_shapes=[
             pltpu.VMEM((NL, 32, HD), F32),
@@ -379,7 +392,10 @@
             pltpu.VMEM((NL, 16, HD), BF16),
             pltpu.VMEM((NL, 16, HD), F32),
             pltpu.VMEM(query.shape, F32),
-            dma((4,)), dma((NZ,)), dma((NZ,)), dma((NL,)), dma((NL,)), dma((2,)), dma((2,)),
+            pltpu.VMEM(query.shape, BF16),
+            pltpu.VMEM(query.shape, F32),
+            pltpu.VMEM(query.shape, F32),
+            dma((3,)), dma((4,)), dma((NZ,)), dma((NZ,)), dma((NL,)), dma((NL,)), dma((2,)), dma((2,)),
             dma((NXY,)), dma((NXY,)), dma((NXY,)), dma((NXY,)), dma((NL,)), dma((NL,)),
         ],
         compiler_params=pltpu.CompilerParams(

time: 50.5 us -> 46.6 us (0.923)
  the two profiles are of different devices: /device:TPU:2 before, /device:TPU:1 now
where the time goes in v3:
time: 46.6 us; the launch traced here: 45.9 us
  Pallas kernels  44.5 us (95%)
  local copies, waits for them, and re-layouts  1.41 us (3%)
    pallas_call x1, Pallas kernels, on_device(): pl.pallas_call(kernel, out_shape=jax.ShapeDtypeStruct(query.shape, BF16),...  44.5 us
    unnamed x1, local copies, waits for them, and re-layouts  1.41 us

profile of v3, /device:TPU:1, one launch (start us, length us, event | category | flops | bytes accessed | tf_op | source)
XLA Modules:
  0.0 45.9 jit_solution(6550609834393338318)
XLA Ops:
  0.0 44.5 %shard_map.55 = bf16[3,5120]{1,0:T(4,128)(2,1)} custom-call(bf16[3,5120]{1,0:T(4,128)(2,1)} %q_ref.1, f32[3,5120]{1,0:T(4,128)} %dk_ref.1, f32[3,5120]{1,0:T(4,128)} %dv_ref.1, bf16[1536,640]{1,0:T(8,128)(2,1)} %bk_ref.1, bf16[1536,640]{1,0:T(8,128)(2,1)} %bv_ref.1), custom_call_target="tpu_custom_call" | custom-call | tf_op jit(solution)/shard_map/pallas_call | solution.py:370
  44.5 1.4 %copy.7 = bf16[3,5120]{1,0:T(4,128)(2,1)} copy(bf16[3,5120]{1,0:T(4,128)(2,1)} %shard_map.55) | data formatting | bytes 61440

commit v4 on v3

v4 whole, which is shorter than its diff:
```python
import math

import jax
import jax.numpy as jnp
from jax import lax
from jax.experimental import pallas as pl
from jax.experimental.pallas import tpu as pltpu
from jax.sharding import PartitionSpec as P

MESH = pl.DeviceIdType.MESH
F32 = jnp.float32
BF16 = jnp.bfloat16

HD = 128
NX, NY, NC = 4, 4, 2
NL = 8
NZ = 2 * NL
GH = 5
GW = GH * HD
TOK = 3
ZT = TOK * NZ
HT = TOK * NL
NXY = NX * NY
PLANE = NXY * NC
KEYS = NC * ZT
NP = NL // 2
SLOTS = 64
QUAD = 4
REACH = (4, -3, 3, -2, 2, -1, 1)
SCALE2 = math.log2(math.e) / math.sqrt(HD)

NT = (((1,), (1,)), ((), ()))


def iota(shape, dim):
    return lax.broadcasted_iota(jnp.int32, shape, dim)


def one_hot(cond):
    return jnp.where(cond, 1.0, 0.0).astype(BF16)


def third(n):
    return jnp.right_shift(n * 43, 7)


def slot_of(r):
    rr = jnp.bitwise_and(r, 15)
    j = third(rr)
    slot = NP * TOK * j + TOK * jnp.right_shift(r, 4) + rr - 3 * j
    return jnp.where(rr < 15, slot, -1)


def place(home, d):
    return lax.rem(d + 3 + jnp.minimum(lax.rem(home + 5, NZ), NL), NL)


def owner_at(home, pos):
    return lax.rem(pos - jnp.minimum(lax.rem(home + 5, NZ), NL) + NL, NL) - 3


def kernel(
    q_ref, dk_ref, dv_ref, bk_ref, bv_ref, out_ref,
    stage, qstage, sbuf, qsend, rbuf, qrecv, pmat, bwin, bf32,
    kall, vall, qall, vt, pbuf, stbuf, obuf, orecv, coef, fbuf, frecv, fstage, fout, q_in, dk_in, dv_in,
    isem, bsem, zs, zr, ws, wr, cs, cr, qs, qr, osm, orm, fs, fr,
):
    p = lax.axis_index("patch")
    h = lax.axis_index("head")
    zh = lax.div(p, PLANE)
    xyc = lax.rem(p, PLANE)
    xy = lax.div(xyc, NC)
    core = lax.rem(xyc, NC)
    z = zh * NL + h

    def zdev(z2):
        return (lax.div(z2, NL) * PLANE + xyc, lax.rem(z2, NL))

    def pfar(k):
        turn_x = lax.div(k, NY)
        turn_y = lax.rem(k, NY)
        x2 = lax.rem(lax.div(xy, NY) + NX // 2 + (2 * lax.rem(turn_x, 2) - 1) * lax.div(turn_x + 1, 2) + NX, NX)
        y2 = lax.rem(lax.rem(xy, NY) + NY // 2 + (2 * lax.rem(turn_y, 2) - 1) * lax.div(turn_y + 1, 2) + NY, NY)
        return x2 * NY + y2

    def pdev(xy2):
        return (zh * PLANE + xy2 * NC + core, h)

    def zfar(k):
        half = lax.div(k + 1, 2)
        return lax.rem(z + NL + (2 * lax.rem(k, 2) - 1) * half + NZ, NZ)

    def near(d):
        return lax.rem(z + d + NZ, NZ)

    def cdev():
        return (zh * PLANE + xy * NC + 1 - core, h)

    barrier = pltpu.get_barrier_semaphore()

    @pl.loop(0, NZ - 1)
    def _(k):
        pl.semaphore_signal(barrier, inc=1, device_id=zdev(zfar(k)), device_id_type=MESH)

    @pl.loop(1, NXY)
    def _(k):
        pl.semaphore_signal(barrier, inc=1, device_id=pdev(lax.rem(xy + k, NXY)), device_id_type=MESH)

    pl.semaphore_signal(barrier, inc=1, device_id=cdev(), device_id_type=MESH)

    base_copies = []
    for a, ref in enumerate((bk_ref, bv_ref)):
        for half in range(2):
            row0 = pl.multiple_of(lax.div(HT * (xyc + half * PLANE), 16) * 16, 16)
            base_copies.append(pltpu.make_async_copy(
                ref.at[pl.ds(row0, 32)], bwin.at[a, half], bsem.at[2 * a + half]))
    in_copies = [
        pltpu.make_async_copy(src, dst, isem.at[n])
        for n, (src, dst) in enumerate(((dk_ref, dk_in), (dv_ref, dv_in), (q_ref, q_in)))]
    for copy in in_copies:
        copy.start()
    for copy in base_copies:
        copy.start()

    lane = iota((TOK, HD), 1)
    sub = iota((TOK, HD), 0)
    for copy in in_copies:
        copy.wait()
    qstage[:, 15:16, :] = jnp.zeros((NL, 1, HD), F32)

    def encode(ref, g):
        block = ref[:, g * HD:(g + 1) * HD]
        scale = (jnp.max(jnp.abs(block), axis=1, keepdims=True) + 1e-06).astype(BF16).astype(F32)
        levels = jnp.floor(127.0 * block / scale + 0.5)
        return jnp.clip(levels, -127.0, 127.0), scale

    for hd in range(NL):
        for a, ref in enumerate((dk_in, dv_in)):
            scales = jnp.zeros((TOK, HD), F32)
            for j in range(GH):
                code, scale = encode(ref, GH * hd + j)
                stage[hd, a, 3 * j:3 * j + 3, :] = code
                scales = jnp.where(lane == 3 * j + sub, scale, scales)
            stage[hd, a, 15:16, :] = jnp.sum(scales, axis=0, keepdims=True)
        sbuf[hd] = stage[hd].astype(BF16)

    for hd in range(NL):
        for j in range(GH):
            g = GH * hd + j
            qstage[hd, 3 * j:3 * j + 3, :] = q_in[:, g * HD:(g + 1) * HD].astype(F32)
    qsend[...] = qstage[...].astype(BF16)

    pl.semaphore_wait(barrier, (NZ - 1) + (NXY - 1) + 1)

    def zcopy(z2, mine, theirs):
        return pltpu.make_async_remote_copy(
            src_ref=sbuf.at[lax.rem(z2, NL)], dst_ref=rbuf.at[mine], send_sem=zs.at[z2], recv_sem=zr.at[theirs],
            device_id=zdev(z2), device_id_type=MESH)

    def wcopy(d):
        z2 = near(-d)
        pos = place(z2, d)
        return pltpu.make_async_remote_copy(
            src_ref=qsend.at[lax.rem(z2, NL)], dst_ref=qrecv.at[pos], send_sem=ws.at[d + 3], recv_sem=wr.at[pos],
            device_id=zdev(z2), device_id_type=MESH)

    def wait_owner(pos):
        pltpu.make_async_remote_copy(
            src_ref=qsend.at[0], dst_ref=qrecv.at[pos], send_sem=ws.at[0], recv_sem=wr.at[pos],
            device_id=zdev(near(1)), device_id_type=MESH).wait_recv()

    for d in REACH:
        wcopy(d).start()

    @pl.loop(0, NZ - 1)
    def _(k):
        zcopy(zfar(k), z, z).start()

    rbuf[z] = sbuf[h]

    own = place(z, 0)
    qrecv[own] = qsend[h]

    col = iota((1, NZ * 16), 1)
    src = jnp.right_shift(col, 4)
    row16 = jnp.bitwise_and(col, 15)
    j_of = third(row16)
    key = ZT * j_of + TOK * src + row16 - 3 * j_of
    key = jnp.where(row16 < 15, key, -1)
    for n in range(GH):
        pmat[n * ZT:(n + 1) * ZT, :] = one_hot(iota((ZT, NZ * 16), 0) + n * ZT == key)
    token = iota((ZT, NZ * 16), 0) - TOK * src
    pmat[GH * ZT:, :] = one_hot((token >= 0) & (token < TOK) & (row16 == 15))
    to_slots = one_hot(iota((SLOTS, NP * 16), 0) == slot_of(iota((SLOTS, NP * 16), 1)))
    to_owners = one_hot(slot_of(iota((NP * 16, SLOTS), 0)) == iota((NP * 16, SLOTS), 1))

    def pcopy(src, dst, xy2, half, theirs, ssem, rsem):
        return pltpu.make_async_remote_copy(
            src_ref=src, dst_ref=dst, send_sem=ssem.at[half, xy2], recv_sem=rsem.at[half, theirs],
            device_id=pdev(xy2), device_id_type=MESH)

    for half in range(2):
        for pos in range(NP * half, NP * half + NP):

            @pl.when(pos != own)
            def _():
                wait_owner(pos)

        qall[half, xy] = jnp.dot(
            to_slots, qrecv[NP * half:NP * half + NP].reshape(NP * 16, HD), preferred_element_type=F32).astype(BF16)

        @pl.loop(0, NXY - 1)
        def _(k):
            pcopy(qall.at[half, xy], qall.at[half, xy], pfar(k), half, xy, qs, qr).start()

    for copy in base_copies:
        copy.wait()
    bf32[...] = bwin[...].astype(F32)

    token_in = iota((ZT, HD), 0)
    lane_of = iota((ZT, HD), 1) - (token_in - 3 * third(token_in))
    ones = jnp.ones((HD, HD), BF16)
    shift = pl.ds(pl.multiple_of(8 * lax.rem(xyc, 2), 8), HT)

    def ccopy(a):
        buf = (kall, vall)[a]
        return pltpu.make_async_remote_copy(
            src_ref=buf.at[core], dst_ref=buf.at[core], send_sem=cs.at[a], recv_sem=cr.at[a],
            device_id=cdev(), device_id_type=MESH)

    @pl.loop(0, NZ - 1)
    def _(k):
        z2 = zfar(NZ - 2 - k)
        zcopy(z2, z, z2).wait_recv()

    def rebuild(a):
        picked = jnp.dot(pmat[...], rbuf[:, a].reshape(NZ * 16, HD), preferred_element_type=F32)
        scales = picked[GH * ZT:]
        by_head = [jnp.where(lane_of == 3 * j, scales, 0.0).astype(BF16) for j in range(GH)]
        steps = jnp.dot(jnp.concatenate(by_head, axis=0), ones, preferred_element_type=F32) / 127.0
        for j in range(GH):
            base = jnp.concatenate(
                [bf32[a, half, shift, j * HD:(j + 1) * HD] for half in range(2)], axis=0)
            rows = slice(j * ZT, (j + 1) * ZT)
            (kall, vall)[a][core, j] = (base + picked[rows] * steps[rows]).astype(BF16)
        ccopy(a).start()

    rebuild(0)
    rebuild(1)
    ccopy(0).wait_recv()

    slot_lane = jnp.bitwise_and(iota((1, QUAD * SLOTS), 1), SLOTS - 1)
    stat_row = iota((8, QUAD * SLOTS), 0)
    last_rows = iota((8, HD), 0) >= 4
    head_slots = NP * TOK

    def weigh(half, first, k):
        for c in range(QUAD):
            tile = first + c

            @pl.when(tile != xy)
            def _():
                pcopy(qall.at[half, tile], qall.at[half, tile], tile, half, tile, qs, qr).wait_recv()

        queries = qall[half, pl.ds(first, QUAD)].reshape(QUAD * SLOTS, HD)
        stacked = lax.dot_general(
            kall[...].reshape(GH * KEYS, HD), queries, NT, preferred_element_type=F32)
        blocks = []
        for c in range(NC):
            block = stacked[(GH * c + GH - 1) * ZT:(GH * c + GH) * ZT]
            for j in range(GH - 2, -1, -1):
                rows = stacked[(GH * c + j) * ZT:(GH * c + j + 1) * ZT]
                block = jnp.where(slot_lane < head_slots * (j + 1), rows, block)
            blocks.append(block)
        scores = jnp.concatenate(blocks, axis=0) * SCALE2
        peak = jnp.max(scores, axis=0, keepdims=True)
        peak_hi = peak.astype(BF16).astype(F32)
        peak_lo = (peak - peak_hi).astype(BF16).astype(F32)
        weights = jnp.exp2(scores - (peak_hi + peak_lo))
        total = jnp.sum(weights, axis=0, keepdims=True)
        total_hi = total.astype(BF16).astype(F32)
        total_lo = total - total_hi
        for c in range(NC):
            for j in range(GH):
                in_head = slot_lane >= head_slots * j
                if j < GH - 1:
                    in_head = in_head & (slot_lane < head_slots * (j + 1))
                n = GH * c + j
                pbuf[k, n * ZT:(n + 1) * ZT, :] = jnp.where(
                    in_head, weights[c * ZT:(c + 1) * ZT], 0.0).astype(BF16)
        stbuf[k] = jnp.where(stat_row == 4, peak_hi, jnp.where(
            stat_row == 5, peak_lo, jnp.where(stat_row == 6, total_hi, total_lo)))

    def mix(half, first, k):
        mixed = jnp.dot(vt[...], pbuf[k], preferred_element_type=F32).T
        for c in range(QUAD):
            part = mixed[c * SLOTS:(c + 1) * SLOTS]
            stat = stbuf[k, :, (c // 2) * HD:(c // 2 + 1) * HD]
            if c % 2:
                stat = pltpu.roll(stat, SLOTS, 1)
            tail = jnp.where(last_rows, stat, part[SLOTS - 8:])
            obuf[half, first + c] = jnp.concatenate([part[:SLOTS - 8], tail], axis=0).astype(BF16)
        for c in range(QUAD):
            tile = first + c

            @pl.when(tile != xy)
            def _():
                pcopy(obuf.at[half, tile], orecv.at[half, xy], tile, half, xy, osm, orm).start()

            @pl.when(tile == xy)
            def _():
                orecv[half, tile] = obuf[half, tile]

    quads = NXY // QUAD

    def quad_at(k):
        turn = (2 * lax.rem(k, 2) - 1) * lax.div(k + 1, 2)
        return QUAD * lax.rem(lax.div(xy, QUAD) + quads // 2 + turn + quads, quads)

    @pl.loop(0, quads // 2)
    def _(k):
        weigh(0, quad_at(k), k)

    ccopy(1).wait_recv()
    eye = one_hot(iota((HD, HD), 0) == iota((HD, HD), 1))
    vt[...] = lax.dot_general(
        eye, vall[...].reshape(GH * KEYS, HD), NT, preferred_element_type=F32).astype(BF16)

    @pl.loop(0, quads // 2)
    def _(k):
        mix(0, quad_at(k), k)

    @pl.loop(quads // 2, quads)
    def _(k):
        weigh(0, quad_at(k), k)
        mix(0, quad_at(k), k)

    @pl.loop(0, quads)
    def _(k):
        weigh(1, quad_at(k), k)

    @pl.loop(0, quads)
    def _(k):
        mix(1, quad_at(k), k)

    def fcopy(pos, theirs):
        return pltpu.make_async_remote_copy(
            src_ref=fbuf.at[pos], dst_ref=frecv.at[h], send_sem=fs.at[pos], recv_sem=fr.at[theirs],
            device_id=zdev(near(owner_at(z, pos))), device_id_type=MESH)

    for half in range(2):

        @pl.loop(1, NXY)
        def _(k):
            xy2 = lax.rem(xy + k, NXY)
            pcopy(obuf.at[half, xy2], orecv.at[half, xy2], xy2, half, xy2, osm, orm).wait_recv()

        stats = [orecv[half, n, SLOTS - 16:SLOTS, :].astype(F32) for n in range(NXY)]
        peaks = [st[12:13] + st[13:14] for st in stats]
        top = peaks[0]
        for n in range(1, NXY):
            top = jnp.maximum(top, peaks[n])
        parts = [jnp.exp2(peaks[n] - top) for n in range(NXY)]
        total = jnp.zeros((1, HD), F32)
        for n in range(NXY):
            total = total + parts[n] * (stats[n][14:15] + stats[n][15:16])
        for n in range(NXY):
            coef[n:n + 1, :] = parts[n] / total
        columns = coef[...].T
        joined = jnp.zeros((SLOTS, HD), F32)
        for n in range(NXY):
            joined = joined + orecv[half, n].astype(F32) * columns[0:SLOTS, n:n + 1]
        owned = jnp.dot(to_owners, joined.astype(BF16), preferred_element_type=F32)
        fbuf[NP * half:NP * half + NP] = owned.astype(BF16).reshape(NP, 16, HD)
        for pos in range(NP * half, NP * half + NP):

            @pl.when(pos != own)
            def _():
                fcopy(pos, h).start()

            @pl.when(pos == own)
            def _():
                frecv[h] = fbuf[pos]

    @pl.loop(0, NZ - 1)
    def _(k):
        zcopy(zfar(k), z, z).wait_send()

    for d in REACH:
        wcopy(d).wait_send()

    for a in range(2):
        ccopy(a).wait_send()

    @pl.loop(1, NXY)
    def _(k):
        xy2 = lax.rem(xy + k, NXY)
        for half in range(2):
            pcopy(qall.at[half, xy], qall.at[half, xy], xy2, half, xy2, qs, qr).wait_send()
            pcopy(obuf.at[half, xy2], orecv.at[half, xy], xy2, half, xy2, osm, orm).wait_send()

    @pl.loop(1, NL)
    def _(k):
        h2 = lax.rem(h + k, NL)
        pltpu.make_async_remote_copy(
            src_ref=fbuf.at[0], dst_ref=frecv.at[h2], send_sem=fs.at[0], recv_sem=fr.at[h2],
            device_id=zdev(near(1)), device_id_type=MESH).wait_recv()

    fstage[...] = frecv[...].astype(F32)
    for hd in range(NL):
        for j in range(GH):
            g = GH * hd + j
            fout[:, g * HD:(g + 1) * HD] = fstage[hd, 3 * j:3 * j + 3, :]
    out_ref[...] = fout[...].astype(BF16)

    for pos in range(NL):

        @pl.when(pos != own)
        def _():
            fcopy(pos, h).wait_send()


def on_device(query, delta_key, delta_value, base_key, base_value):
    vmem = pl.BlockSpec(memory_space=pltpu.VMEM)
    hbm = pl.BlockSpec(memory_space=pl.ANY)
    dma = pltpu.SemaphoreType.DMA
    return pl.pallas_call(
        kernel,
        out_shape=jax.ShapeDtypeStruct(query.shape, BF16),
        in_specs=[hbm] * 5,
        out_specs=vmem,
        scratch_shapes=[
            pltpu.VMEM((NL, 2, 16, HD), F32),
            pltpu.VMEM((NL, 16, HD), F32),
            pltpu.VMEM((NL, 2, 16, HD), BF16),
            pltpu.VMEM((NL, 16, HD), BF16),
            pltpu.VMEM((NZ, 2, 16, HD), BF16),
            pltpu.VMEM((NL, 16, HD), BF16),
            pltpu.VMEM(((GH + 1) * ZT, NZ * 16), BF16),
            pltpu.VMEM((2, 2, 32, GW), BF16),
            pltpu.VMEM((2, 2, 32, GW), F32),
            pltpu.VMEM((NC, GH, ZT, HD), BF16),
            pltpu.VMEM((NC, GH, ZT, HD), BF16),
            pltpu.VMEM((2, NXY, SLOTS, HD), BF16),
            pltpu.VMEM((HD, GH * KEYS), BF16),
            pltpu.VMEM((NXY // QUAD, GH * KEYS, QUAD * SLOTS), BF16),
            pltpu.VMEM((NXY // QUAD, 8, QUAD * SLOTS), F32),
            pltpu.VMEM((2, NXY, SLOTS, HD), BF16),
            pltpu.VMEM((2, NXY, SLOTS, HD), BF16),
            pltpu.VMEM((NXY, HD), F32),
            pltpu.VMEM((NL, 16, HD), BF16),
            pltpu.VMEM((NL, 16, HD), BF16),
            pltpu.VMEM((NL, 16, HD), F32),
            pltpu.VMEM(query.shape, F32),
            pltpu.VMEM(query.shape, BF16),
            pltpu.VMEM(query.shape, F32),
            pltpu.VMEM(query.shape, F32),
            dma((3,)), dma((4,)), dma((NZ,)), dma((NZ,)), dma((NL,)), dma((NL,)), dma((2,)), dma((2,)),
            dma((2, NXY)), dma((2, NXY)), dma((2, NXY)), dma((2, NXY)), dma((NL,)), dma((NL,)),
        ],
        compiler_params=pltpu.CompilerParams(
            collective_id=0, has_side_effects=True, vmem_limit_bytes=60 * 1024 * 1024),
    )(query, delta_key, delta_value, base_key, base_value)


def solution(mesh):
    rows = P(("patch", "head"), None)
    cols = P(None, "head")
    return jax.shard_map(
        on_device, mesh=mesh, in_specs=(rows, rows, rows, cols, cols), out_specs=rows, check_vma=False)
```

time: 46.6 us -> 44.6 us (0.957)
  Pallas kernels: 44.5 us -> 42.3 us
    pallas_call x1, Pallas kernels: 44.5 us -> 42.3 us  [on_device(): pl.pallas_call(kernel, out_shape=jax.ShapeDtypeStruct(query.shape, BF16),...]
where the time goes in v4:
time: 44.6 us; the launch traced here: 43.7 us
  Pallas kernels  42.3 us (95%)
  local copies, waits for them, and re-layouts  1.41 us (3%)
    pallas_call x1, Pallas kernels, on_device(): pl.pallas_call(kernel, out_shape=jax.ShapeDtypeStruct(query.shape, BF16),...  42.3 us
    unnamed x1, local copies, waits for them, and re-layouts  1.41 us

profile of v4, /device:TPU:1, one launch (start us, length us, event | category | flops | bytes accessed | tf_op | source)
XLA Modules:
  0.0 43.7 jit_solution(3919160991367440025)
XLA Ops:
  0.0 42.3 %shard_map.55 = bf16[3,5120]{1,0:T(4,128)(2,1)} custom-call(bf16[3,5120]{1,0:T(4,128)(2,1)} %q_ref.1, f32[3,5120]{1,0:T(4,128)} %dk_ref.1, f32[3,5120]{1,0:T(4,128)} %dv_ref.1, bf16[1536,640]{1,0:T(8,128)(2,1)} %bk_ref.1, bf16[1536,640]{1,0:T(8,128)(2,1)} %bv_ref.1), custom_call_target="tpu_custom_call" | custom-call | tf_op jit(solution)/shard_map/pallas_call | solution.py:427
  42.3 1.4 %copy.7 = bf16[3,5120]{1,0:T(4,128)(2,1)} copy(bf16[3,5120]{1,0:T(4,128)(2,1)} %shard_map.55) | data formatting | bytes 61440

commit v5 on v4

--- a/solution.py
+++ b/solution.py
@@ -301,7 +301,7 @@
             tail = jnp.where(last_rows, stat, part[SLOTS - 8:])
             obuf[half, first + c] = jnp.concatenate([part[:SLOTS - 8], tail], axis=0).astype(BF16)
         for c in range(QUAD):
-            tile = first + c
+            tile = first + lax.rem(xy + (2, 1, 3, 0)[c], QUAD)
 
             @pl.when(tile != xy)
             def _():

time: 44.6 us -> 44.1 us (0.989); the launches traced: 43.7 us -> 43.9 us
  no operation moved by 1% of the time
where the time goes in v5:
time: 44.1 us; the launch traced here: 43.9 us
  Pallas kernels  42.5 us (96%)
  local copies, waits for them, and re-layouts  1.41 us (3%)
    pallas_call x1, Pallas kernels, on_device(): pl.pallas_call(kernel, out_shape=jax.ShapeDtypeStruct(query.shape, BF16),...  42.5 us
    unnamed x1, local copies, waits for them, and re-layouts  1.41 us

profile of v5, /device:TPU:1, one launch (start us, length us, event | category | flops | bytes accessed | tf_op | source)
XLA Modules:
  0.0 43.9 jit_solution(15873397748156960550)
XLA Ops:
  0.0 42.5 %shard_map.55 = bf16[3,5120]{1,0:T(4,128)(2,1)} custom-call(bf16[3,5120]{1,0:T(4,128)(2,1)} %q_ref.1, f32[3,5120]{1,0:T(4,128)} %dk_ref.1, f32[3,5120]{1,0:T(4,128)} %dv_ref.1, bf16[1536,640]{1,0:T(8,128)(2,1)} %bk_ref.1, bf16[1536,640]{1,0:T(8,128)(2,1)} %bv_ref.1), custom_call_target="tpu_custom_call" | custom-call | tf_op jit(solution)/shard_map/pallas_call | solution.py:427
  42.5 1.4 %copy.7 = bf16[3,5120]{1,0:T(4,128)(2,1)} copy(bf16[3,5120]{1,0:T(4,128)(2,1)} %shard_map.55) | data formatting | bytes 61440

commit v6 on v5

--- a/solution.py
+++ b/solution.py
@@ -317,7 +317,7 @@
         turn = (2 * lax.rem(k, 2) - 1) * lax.div(k + 1, 2)
         return QUAD * lax.rem(lax.div(xy, QUAD) + quads // 2 + turn + quads, quads)
 
-    @pl.loop(0, quads // 2)
+    @pl.loop(0, 3)
     def _(k):
         weigh(0, quad_at(k), k)
 
@@ -326,11 +326,11 @@
     vt[...] = lax.dot_general(
         eye, vall[...].reshape(GH * KEYS, HD), NT, preferred_element_type=F32).astype(BF16)
 
-    @pl.loop(0, quads // 2)
+    @pl.loop(0, 3)
     def _(k):
         mix(0, quad_at(k), k)
 
-    @pl.loop(quads // 2, quads)
+    @pl.loop(3, quads)
     def _(k):
         weigh(0, quad_at(k), k)
         mix(0, quad_at(k), k)
@@ -382,6 +382,14 @@
             def _():
                 frecv[h] = fbuf[pos]
 
+    def assemble(h2):
+        fstage[h2] = frecv[h2].astype(F32)
+        for j in range(GH):
+            columns = pl.ds(pl.multiple_of(h2 * GW + j * HD, HD), HD)
+            fout[:, columns] = fstage[h2, 3 * j:3 * j + 3, :]
+
+    assemble(h)
+
     @pl.loop(0, NZ - 1)
     def _(k):
         zcopy(zfar(k), z, z).wait_send()
@@ -399,18 +407,13 @@
             pcopy(qall.at[half, xy], qall.at[half, xy], xy2, half, xy2, qs, qr).wait_send()
             pcopy(obuf.at[half, xy2], orecv.at[half, xy], xy2, half, xy2, osm, orm).wait_send()
 
-    @pl.loop(1, NL)
-    def _(k):
-        h2 = lax.rem(h + k, NL)
+    for d in reversed(REACH):
+        h2 = lax.rem(near(-d), NL)
         pltpu.make_async_remote_copy(
             src_ref=fbuf.at[0], dst_ref=frecv.at[h2], send_sem=fs.at[0], recv_sem=fr.at[h2],
             device_id=zdev(near(1)), device_id_type=MESH).wait_recv()
-
-    fstage[...] = frecv[...].astype(F32)
-    for hd in range(NL):
-        for j in range(GH):
-            g = GH * hd + j
-            fout[:, g * HD:(g + 1) * HD] = fstage[hd, 3 * j:3 * j + 3, :]
+        assemble(h2)
+
     out_ref[...] = fout[...].astype(BF16)
 
     for pos in range(NL):

time: 44.1 us -> 44.3 us (level)
  no operation moved by 1% of the time
where the time goes in v6:
time: 44.3 us; the launch traced here: 43.8 us
  Pallas kernels  42.4 us (96%)
  local copies, waits for them, and re-layouts  1.41 us (3%)
    pallas_call x1, Pallas kernels, on_device(): pl.pallas_call(kernel, out_shape=jax.ShapeDtypeStruct(query.shape, BF16),...  42.4 us
    unnamed x1, local copies, waits for them, and re-layouts  1.41 us

profile of v6, /device:TPU:1, one launch (start us, length us, event | category | flops | bytes accessed | tf_op | source)
XLA Modules:
  0.0 43.8 jit_solution(6269525590806101478)
XLA Ops:
  0.0 42.4 %shard_map.55 = bf16[3,5120]{1,0:T(4,128)(2,1)} custom-call(bf16[3,5120]{1,0:T(4,128)(2,1)} %q_ref.1, f32[3,5120]{1,0:T(4,128)} %dk_ref.1, f32[3,5120]{1,0:T(4,128)} %dv_ref.1, bf16[1536,640]{1,0:T(8,128)(2,1)} %bk_ref.1, bf16[1536,640]{1,0:T(8,128)(2,1)} %bv_ref.1), custom_call_target="tpu_custom_call" | custom-call | tf_op jit(solution)/shard_map/pallas_call | solution.py:430
  42.4 1.4 %copy.7 = bf16[3,5120]{1,0:T(4,128)(2,1)} copy(bf16[3,5120]{1,0:T(4,128)(2,1)} %shard_map.55) | data formatting | bytes 61440
